TPU v7x, 128 devices: a whole 4x4x4 slice. The times are simulated.
128 devices in a mesh: nodes: 32 (over y, z, core), feat: 4 (over x).
Axes of the slice: x: 4, y: 4, z: 4, core: 2. Of those that a mesh axis runs over, the one named last changes fastest.
Arguments:
- features: bfloat16 [131072, 1024], P('nodes', 'feat'), may hold values from -6 to 6
- pair_count: int32 [32, 32], P('nodes'), may hold values from 1 to 2, as said below
- send_blocks: int32 [32, 32, 2], P('nodes'), may hold values from 0 to 31
- tile_src: int32 [1024, 4], P('nodes'), may hold values from 0 to 63, as said below
- tiles: bfloat16 [1024, 4, 128, 128], P('nodes'), may hold values from -0.25 to 0.25
- labels: int32 [131072], P('nodes'), may hold values from 0 to 15
- w_first: bfloat16 [1024, 1024], P('feat'), may hold values from -0.1875 to 0.1875
- b_first: float32 [1024], P('feat'), may hold values from -3 to 3
- w_second: bfloat16 [1024, 16], P('feat'), may hold values from -0.1875 to 0.1875
Outputs:
- grad_first: float32 [1024, 1024], P('feat', 'nodes')
- grad_bias: float32 [1024], P('feat')
- grad_second: float32 [1024, 16], P('feat')
Inputs may be any that keep to these rules, and one draw needn't show every extreme that they name: pair_count[p, p] is 2 for every p. `tile_src`: the 32 rows of one partition name every slot 0 to 63 at least once.
All inputs are finite; a program needn't handle non-finite values.
Results may differ from a plain program's by a relative error of at most 0.015.
The roundings to bfloat16 on the way count: a program that leaves them out, or rounds other values in their place, can miss the bound.
Values may be sent and summed in bfloat16 or wider, within the bound.
No kernel may reach another device: no remote copies, remote signals or barrier semaphores. Data moves between devices by JAX's collectives and lax.ppermute only.
A program may use at most 128 MiB of HBM per device.

v0:
```python
import math
import jax
import jax.numpy as jnp
from jax import lax
from jax.sharding import PartitionSpec as P


def shards(features, pair_count, send_blocks, tile_src, tiles, labels, w_first, b_first, w_second):
    high = lax.Precision.HIGHEST
    rows, width = features.shape
    nblocks, per_block = tile_src.shape
    blk = tiles.shape[2]
    parts = lax.axis_size("nodes")
    slots = send_blocks.shape[2]
    grades = w_second.shape[1]
    hq = w_first.shape[1] // lax.axis_size("feat")
    owner = tile_src // slots
    slot_in = tile_src % slots
    counts = pair_count[0]
    live = slot_in < counts[owner]
    weights = tiles * live[:, :, None, None].astype(jnp.bfloat16)
    table = send_blocks[0]

    def gather_sources(received):
        flat = received.reshape(parts * slots, blk, received.shape[-1])
        return flat[tile_src]

    own_one = features.reshape(nblocks, blk, width)
    arrived = lax.all_to_all(own_one[table], "nodes", split_axis=0, concat_axis=0, tiled=True)
    summed = jnp.einsum(
        "btij,btjf->bif", weights, gather_sources(arrived), preferred_element_type=jnp.float32
    )
    agg_first = (summed + own_one).astype(jnp.bfloat16).reshape(rows, width)
    partial_pre = jnp.dot(agg_first, w_first, preferred_element_type=jnp.float32)
    pre = lax.psum_scatter(partial_pre, "feat", scatter_dimension=1, tiled=True)
    pre = pre + b_first
    hidden = jnp.maximum(pre, 0.0).astype(jnp.bfloat16)
    own_two = hidden.reshape(nblocks, blk, hq)
    arrived_two = lax.all_to_all(own_two[table], "nodes", split_axis=0, concat_axis=0, tiled=True)
    agg_second = (
        jnp.einsum(
            "btij,btjf->bif",
            weights,
            gather_sources(arrived_two),
            preferred_element_type=jnp.float32,
        )
        + own_two
    )
    partial_logits = jnp.dot(
        agg_second.reshape(rows, hq), w_second.astype(jnp.float32), precision=high
    )
    logits = lax.psum(partial_logits, "feat")
    expo = jnp.exp(logits)
    probs = expo / jnp.sum(expo, axis=1, keepdims=True)
    onehot = (labels[:, None] == jnp.arange(grades, dtype=jnp.int32)[None, :]).astype(jnp.float32)
    dlog = (probs - onehot) * (1.0 / math.sqrt(rows * parts))
    dlog_b = dlog.astype(jnp.bfloat16).reshape(nblocks, blk, grades)
    contrib = jnp.einsum("btij,bif->btjf", weights, dlog_b, preferred_element_type=jnp.float32)
    slot_hit = (
        tile_src.reshape(-1)[:, None] == jnp.arange(parts * slots, dtype=jnp.int32)[None, :]
    ).astype(jnp.float32)
    slotsum = lax.dot_general(
        slot_hit,
        contrib.reshape(nblocks * per_block, blk * grades),
        (((0,), (0,)), ((), ())),
        precision=high,
    )
    returned = lax.all_to_all(
        slotsum.reshape(parts, slots, blk, grades).astype(jnp.bfloat16),
        "nodes",
        split_axis=0,
        concat_axis=0,
        tiled=True,
    ).astype(jnp.float32)
    placing = (table.reshape(-1)[None, :] == jnp.arange(nblocks, dtype=jnp.int32)[:, None]).astype(
        jnp.float32
    )
    spread = jnp.dot(placing, returned.reshape(parts * slots, blk * grades), precision=high)
    dproj_b = (dlog + spread.reshape(rows, grades)).astype(jnp.bfloat16)
    grad_second = lax.dot_general(
        hidden, dproj_b, (((0,), (0,)), ((), ())), preferred_element_type=jnp.float32
    )
    dhid = lax.dot_general(
        dproj_b, w_second, (((1,), (1,)), ((), ())), preferred_element_type=jnp.float32
    )
    dpre = jnp.where(pre > 0, dhid, 0.0)
    grad_bias = jnp.sum(dpre, axis=0)
    grad_second, grad_bias = lax.psum((grad_second, grad_bias), "nodes")
    dpre_b = dpre.astype(jnp.bfloat16)
    grad_part = lax.dot_general(
        agg_first,
        lax.all_gather(dpre_b, "feat", axis=1, tiled=True),
        (((0,), (0,)), ((), ())),
        preferred_element_type=jnp.float32,
    )
    grad_first = lax.psum_scatter(
        grad_part.astype(jnp.bfloat16), "nodes", scatter_dimension=1, tiled=True
    ).astype(jnp.float32)
    return (grad_first, grad_bias, grad_second)


def solution(mesh):
    placed = (
        P("nodes", "feat"),
        P("nodes", None),
        P("nodes", None, None),
        P("nodes", None),
        P("nodes", None, None, None),
        P("nodes"),
        P("feat", None),
        P("feat"),
        P("feat", None),
    )
    return jax.shard_map(
        shards,
        mesh=mesh,
        in_specs=placed,
        out_specs=(P("feat", "nodes"), P("feat"), P("feat", None)),
        check_vma=False,
    )
```

profile of v0, /device:TPU:0, one launch (start us, length us, event | category | flops | bytes accessed | tf_op | source)
XLA Modules:
  0.0 650.3 jit_solution(7798856695492343430)
XLA Ops:
  7.2 0.0 copy-start
  7.2 0.7 compare_select_fusion.1
  7.9 0.1 copy.59
  8.0 0.1 reshape.111
  8.1 4.4 gather_fusion.1
  12.5 8.7 %all-to-all-start = ((bf16[32,2,128,256]{3,2,1,0:T(8,128)(2,1)}), bf16[32,2,128,256]{3,2,1,0:T(8,128)(2,1)}, u32[]{:S(2)}, u32[]{:S(2)}) async-start(bf16[32,2,128,256]{3,2,1,0:T(8,128)(2,1)} %bitcast.63), calls=%async_computation | async-start | bytes 8388608 | tf_op jit(solution)/shard_map/all_to_all | solution.py:29
  21.2 0.0 reduce-scatter.3.cloned.1.call-start
  21.2 0.0 copy-done.8
  21.3 0.1 copy.60
  21.3 0.1 reshape.119
  21.5 0.1 copy.56
  21.5 0.1 reshape.103
  21.7 1.2 gather_fusion
  22.9 0.1 reshape.102
  23.0 0.1 copy.57
  23.1 0.1 copy.58
  23.2 50.7 %all-to-all-done = bf16[32,2,128,256]{3,2,1,0:T(8,128)(2,1)} async-done(((bf16[32,2,128,256]{3,2,1,0:T(8,128)(2,1)}), bf16[32,2,128,256]{3,2,1,0:T(8,128)(2,1)}, u32[]{:S(2)}, u32[]{:S(2)}) %all-to-all-start) | async-done | bytes 4194336 | tf_op jit(solution)/shard_map/all_to_all | solution.py:29
  74.0 8.9 %gather_fusion.2 = bf16[128,128,256]{2,1,0:T(8,128)(2,1)} fusion(bf16[64,128,256]{2,1,0:T(8,128)(2,1)} %bitcast.4, s32[1024]{0:T(1024)S(1)} %pad_clamp_fusion), kind=kCustom, calls=%fused_computation.2 | custom fusion | bytes 16777728 | tf_op jit(solution)/shard_map/gather | solution.py:26
  82.9 6.5 fusion
  89.3 1.3 copy-done.5
  90.6 8.1 %fusion.27 = f32[4096,1024]{1,0:T(8,128)} fusion(bf16[4096,256]{1,0:T(8,128)(2,1)S(1)} %bitcast.70, bf16[256,1024]{1,0:T(8,128)(2,1)S(1)} %copy-done), kind=kOutput, calls=%fused_computation.54 | convolution fusion | flops 2147483648 | bytes 19398656 | tf_op jit(solution)/shard_map/dot_general | solution.py:34
  98.7 0.0 reduce-scatter.3.cloned.1.call-update
  98.8 0.0 all-reduce.3.cloned.1.call-start
  98.8 148.5 %reduce-scatter.3.cloned.1.call-done = f32[4096,256]{1,0:T(8,128)} async-done(((f32[4096,1024]{1,0:T(8,128)}), f32[4096,256]{1,0:T(8,128)}) %reduce-scatter.3.cloned.1.call-update) | async-done | bytes 4194320 | tf_op jit(solution)/shard_map/reduce_scatter | solution.py:35
  247.3 2.6 maximum_convert_fusion
  249.9 2.7 gather_fusion.3
  252.6 57.9 %all_to_all.15 = bf16[32,2,128,256]{3,2,1,0:T(8,128)(2,1)} all-to-all(bf16[32,2,128,256]{3,2,1,0:T(8,128)(2,1)} %bitcast.64), channel_id=1, replica_groups=mesh['nodes'=32,'feat'=4] {'nodes'}, dimensions={0} | all-to-all | bytes 8388608 | tf_op jit(solution)/shard_map/all_to_all | solution.py:39
  310.5 8.8 %gather_fusion.4 = bf16[128,128,256]{2,1,0:T(8,128)(2,1)} fusion(bf16[64,128,256]{2,1,0:T(8,128)(2,1)} %bitcast.61, s32[1024]{0:T(1024)S(1)} %pad_clamp_fusion), kind=kCustom, calls=%fused_computation.4 | custom fusion | bytes 16777728 | tf_op jit(solution)/shard_map/gather | solution.py:26
  319.3 6.5 bitcast_add_fusion
  325.8 0.0 copy-start.6
  325.8 2.7 fusion.28
  328.5 0.0 all-reduce.3.cloned.1.call-update
  328.6 0.1 copy.62
  328.6 0.1 eq.68
  328.8 38.1 %all-reduce.3.cloned.1.call-done = f32[4096,16]{0,1:T(8,128)} async-done(((f32[4096,16]{0,1:T(8,128)}), f32[4096,16]{0,1:T(8,128)}) %all-reduce.3.cloned.1.call-update) | async-done | bytes 262160 | tf_op jit(solution)/shard_map/psum | solution.py:52
  366.8 1.0 exponential_reduce_fusion
  367.9 0.0 copy-done.6
  367.9 1.0 convert_bitcast_fusion
  368.9 6.9 %fusion.1 = f32[32,4,128,16]{3,2,1,0:T(8,128)} fusion(bf16[32,4,128,128]{3,2,1,0:T(8,128)(2,1)} %param.13, bf16[32,4]{1,0:T(8,128)(2,1)S(1)} %copy.58, bf16[32,128,16,1]{1,0,2,3:T(8,128)(2,1)S(1)} %bitcast.72), kind=kOutput, calls=%fused_computation.10 | convolution fusion | flops 69206016 | bytes 5374208 | tf_op jit(solution)/shard_map/btij,bif->btjf/dot_general | solution.py:58
  375.8 8.7 %reshape.98 = f32[128,2048]{1,0:T(8,128)} reshape(f32[32,4,128,16]{3,2,1,0:T(8,128)} %fusion.1) | data formatting | bytes 2097152 | tf_op jit(solution)/shard_map/reshape | solution.py:64
  384.5 2.5 copy.65
  387.0 2.2 convolution_convert_fusion.1
  389.3 0.8 copy.67
  390.1 7.3 %all-to-all-start.2 = ((bf16[32,2,128,16]{2,3,1,0:T(8,128)(2,1)}), bf16[32,2,128,16]{2,3,1,0:T(8,128)(2,1)S(1)}, u32[]{:S(2)}, u32[]{:S(2)}) async-start(bf16[32,2,128,16]{2,3,1,0:T(8,128)(2,1)} %copy.67), calls=%async_computation.3 | async-start | bytes 524288 | tf_op jit(solution)/shard_map/all_to_all | solution.py:68
  397.3 0.3 all-gather.2.cloned.1.call-start
  397.6 0.1 copy.61
  397.7 0.1 eq.64
  397.8 8.5 %all-to-all-done.2 = bf16[32,2,128,16]{2,3,1,0:T(8,128)(2,1)S(1)} async-done(((bf16[32,2,128,16]{2,3,1,0:T(8,128)(2,1)}), bf16[32,2,128,16]{2,3,1,0:T(8,128)(2,1)S(1)}, u32[]{:S(2)}, u32[]{:S(2)}) %all-to-all-start.2) | async-done | bytes 262176 | tf_op jit(solution)/shard_map/all_to_all | solution.py:68
  406.3 1.7 copy.68
  408.0 4.7 reshape.99
  412.8 0.2 fusion.21
  412.9 2.1 reshape.100
  415.0 2.2 copy.69
  417.1 0.0 copy-done.4
  417.2 0.1 add_convert_fusion
  417.3 4.5 fusion.26
  421.7 0.0 all-gather.2.cloned.1.call-update
  421.8 0.0 reduce-scatter.5.cloned.1.call-start
  421.8 84.4 %all-gather.2.cloned.1.call-done = bf16[4096,1024]{1,0:T(8,128)(2,1)} async-done(((bf16[4096,256]{1,0:T(8,128)(2,1)}), bf16[4096,1024]{1,0:T(8,128)(2,1)}) %all-gather.2.cloned.1.call-update) | async-done | bytes 8388624 | tf_op jit(solution)/shard_map/all_gather | solution.py:92
  506.3 8.2 %convolution_convert_fusion = bf16[256,1024]{0,1:T(8,128)(2,1)} fusion(bf16[4096,256]{1,0:T(8,128)(2,1)} %bitcast.71, bf16[4096,1024]{1,0:T(8,128)(2,1)} %all-gather.2.cloned.1.call-done), kind=kOutput, calls=%fused_computation.19 | convolution fusion | flops 2147745792 | bytes 11010048 | tf_op jit(solution)/shard_map/dot_general | solution.py:90
  514.5 0.0 reduce-scatter.5.cloned.1.call-update
  514.5 0.4 fusion.29
  514.9 127.5 %all-reduce = (f32[256]{0:T(256)}, f32[256,16]{0,1:T(8,128)}) all-reduce(f32[256]{0:T(256)S(1)} %get-tuple-element.5, f32[256,16]{0,1:T(8,128)S(1)} %fusion.29), channel_id=1, replica_groups=mesh['nodes'=32,'feat'=4] {'nodes'}, use_global_device_ids=true, to_apply=%region_5.6 | all-reduce | flops 4352 | bytes 34816 | tf_op jit(solution)/shard_map/psum | solution.py:88
  642.4 1.3 convert_element_type.52
  (24 shorter events, 0.1 us)
Async XLA Ops:
  7.2 83.5 %copy-start = (bf16[256,1024]{1,0:T(8,128)(2,1)S(1)}, bf16[256,1024]{1,0:T(8,128)(2,1)}, u32[]{:S(2)}) copy-start(bf16[256,1024]{1,0:T(8,128)(2,1)} %param.15) | copy-start | bytes 1572868
  12.5 8.7 %copy-start.8 = (s32[32,4]{0,1:T(4,128)S(1)}, s32[32,4]{0,1:T(4,128)}, u32[]{:S(2)}) copy-start(s32[32,4]{0,1:T(4,128)} %param.12) | copy-start | bytes 1540
  12.5 9.2 %copy-start.2 = (s32[1,32]{1,0:T(1,128)S(1)}, s32[1,32]{1,0:T(1,128)}, u32[]{:S(2)}) copy-start(s32[1,32]{1,0:T(1,128)} %param.10) | copy-start | bytes 388
  12.5 61.5 %all-to-all-start = ((bf16[32,2,128,256]{3,2,1,0:T(8,128)(2,1)}), bf16[32,2,128,256]{3,2,1,0:T(8,128)(2,1)}, u32[]{:S(2)}, u32[]{:S(2)}) async-start(bf16[32,2,128,256]{3,2,1,0:T(8,128)(2,1)} %bitcast.63), calls=%async_computation | async-start | bytes 8388608 | tf_op jit(solution)/shard_map/all_to_all | solution.py:29
  21.2 226.1 %reduce-scatter.3.cloned.1.call-start = ((), (), s32[]{:S(2)}) async-start(), calls=%async_computation.5 | async-start | bytes 20971520 | tf_op jit(solution)/shard_map/reduce_scatter | solution.py:35
  74.0 8.9 %copy-start.3 = (bf16[4096,256]{1,0:T(8,128)(2,1)S(1)}, bf16[4096,256]{1,0:T(8,128)(2,1)}, u32[]{:S(2)}) copy-start(bf16[4096,256]{1,0:T(8,128)(2,1)} %param.9) | copy-start | bytes 6291460
  89.3 1.3 copy-start.5
  98.7 148.6 %copy-start.10 = (f32[256]{0:T(256)S(1)}, f32[256]{0:T(256)}, u32[]{:S(2)}) copy-start(f32[256]{0:T(256)} %param.16) | copy-start | bytes 3076
  98.8 268.1 %all-reduce.3.cloned.1.call-start = ((), (), s32[]{:S(2)}) async-start(), calls=%async_computation.6 | async-start | bytes 524288 | tf_op jit(solution)/shard_map/psum | solution.py:52
  319.3 6.5 %copy-start.7 = (bf16[256,16]{0,1:T(8,128)(2,1)S(1)}, bf16[256,16]{0,1:T(8,128)(2,1)}, u32[]{:S(2)}) copy-start(bf16[256,16]{0,1:T(8,128)(2,1)} %param.17) | copy-start | bytes 24580
  325.8 42.1 %copy-start.6 = (s32[4096]{0:T(1024)S(1)}, s32[4096]{0:T(1024)}, u32[]{:S(2)}) copy-start(s32[4096]{0:T(1024)} %param.14) | copy-start | bytes 49156
  384.5 13.1 %copy-start.9 = (s32[1,32,2]{1,2,0:T(2,128)S(1)}, s32[1,32,2]{1,2,0:T(2,128)}, u32[]{:S(2)}) copy-start(s32[1,32,2]{1,2,0:T(2,128)} %param.11) | copy-start | bytes 772
  390.1 16.2 %all-to-all-start.2 = ((bf16[32,2,128,16]{2,3,1,0:T(8,128)(2,1)}), bf16[32,2,128,16]{2,3,1,0:T(8,128)(2,1)S(1)}, u32[]{:S(2)}, u32[]{:S(2)}) async-start(bf16[32,2,128,16]{2,3,1,0:T(8,128)(2,1)} %copy.67), calls=%async_computation.3 | async-start | bytes 524288 | tf_op jit(solution)/shard_map/all_to_all | solution.py:68
  397.3 108.9 %all-gather.2.cloned.1.call-start = ((), (), s32[]{:S(2)}) async-start(), calls=%async_computation.7 | async-start | bytes 10485760 | tf_op jit(solution)/shard_map/all_gather | solution.py:92
  408.0 9.1 %copy-start.4 = (f32[4096,16]{0,1:T(8,128)S(1)}, f32[4096,16]{0,1:T(8,128)}, u32[]{:S(2)}) copy-start(f32[4096,16]{0,1:T(8,128)} %all-reduce.3.cloned.1.call-done) | copy-start | bytes 786436
  421.8 220.6 %reduce-scatter.5.cloned.1.call-start = ((), (), s32[]{:S(2)}) async-start(), calls=%async_computation.8 | async-start | bytes 540672 | tf_op jit(solution)/shard_map/reduce_scatter | solution.py:96
  506.3 137.5 %copy-start.1 = (bf16[256,1024]{1,0:T(8,128)(2,1)S(1)}, bf16[256,1024]{1,0:T(8,128)(2,1)}, u32[]{:S(2)}) copy-start(bf16[256,1024]{1,0:T(8,128)(2,1)} %param.15) | copy-start | bytes 1572868
Sparse Core Ops, SparseCore 0:
  98.9 148.3 reduce-scatter.2
  328.7 38.1 all-reduce.2
  421.9 84.3 all-gather.1
  514.7 77.6 reduce-scatter.4
where the time goes:
time: 651 us; the launch traced here: 650 us
  waiting for transfers between devices  330 us (51%)
  blocking collectives  185 us (28%)
  local copies, waits for them, and re-layouts  51.3 us (8%)
  matrix products  46.1 us (7%)
  starting transfers between devices  16.3 us (3%)
  between operations  14 us (2%)
  other arithmetic  6.85 us (1%)
    reduce_scatter x1, waiting for transfers between devices, shards(): pre = lax.psum_scatter(partial_pre, 'feat', scatter_dimension=1, tiled=True)  149 us
    psum x1, blocking collectives, shards(): grad_second, grad_bias = lax.psum((grad_second, grad_bias), 'nodes')  127 us
    all_gather x1, waiting for transfers between devices, shards(): lax.all_gather(dpre_b, 'feat', axis=1, tiled=True)  84.4 us
    all_to_all x1, blocking collectives, shards(): lax.all_to_all(own_two[table], 'nodes', split_axis=0, concat_axis=0, tile...  57.9 us
    all_to_all x1, waiting for transfers between devices, shards(): lax.all_to_all(own_one[table], 'nodes', split_axis=0, concat_axis=0, tile...  50.7 us
    psum x1, waiting for transfers between devices, shards(): logits = lax.psum(partial_logits, 'feat')  38.1 us
    gather x2, local copies, waits for them, and re-layouts, gather_sources(): return flat[tile_src]  17.6 us
  transfers between devices with their start and end apart: 6, of which 5 were waited for; matrix products, arithmetic and copies ran while one was open for 0% of the time, Pallas kernels for 0%

commit v1 on v0

--- a/solution.py
+++ b/solution.py
@@ -49,7 +49,9 @@
     partial_logits = jnp.dot(
         agg_second.reshape(rows, hq), w_second.astype(jnp.float32), precision=high
     )
-    logits = lax.psum(partial_logits, "feat")
+    logits = partial_logits
+    for hop in (1, 2):
+        logits = logits + lax.ppermute(logits, "feat", [(dev, dev ^ hop) for dev in range(4)])
     expo = jnp.exp(logits)
     probs = expo / jnp.sum(expo, axis=1, keepdims=True)
     onehot = (labels[:, None] == jnp.arange(grades, dtype=jnp.int32)[None, :]).astype(jnp.float32)

time: 651 us -> 624 us (0.959)
  waiting for transfers between devices: 330 us -> 307 us
    psum x1 -> x0, waiting for transfers between devices: 38.1 us -> none  [shards(): logits = lax.psum(partial_logits, 'feat')]
    ppermute x0 -> x2, waiting for transfers between devices: none -> 15.9 us  [shards(): lax.ppermute(logits, 'feat', [(dev, dev ^ hop) for dev in range(4)])]
  transfers between devices with their start and end apart: 6 -> 7, of which waited for: 5 -> 6; matrix products, arithmetic and copies ran while one was open for 0% -> 0% of each run, Pallas kernels for 0% -> 0%
where the time goes in v1:
time: 624 us; the launch traced here: 623 us
  waiting for transfers between devices  307 us (49%)
  blocking collectives  185 us (30%)
  local copies, waits for them, and re-layouts  51.3 us (8%)
  matrix products  45.4 us (7%)
  starting transfers between devices  14.7 us (2%)
  between operations  14 us (2%)
    reduce_scatter x1, waiting for transfers between devices, shards(): pre = lax.psum_scatter(partial_pre, 'feat', scatter_dimension=1, tiled=True)  149 us
    psum x1, blocking collectives, shards(): grad_second, grad_bias = lax.psum((grad_second, grad_bias), 'nodes')  127 us
    all_gather x1, waiting for transfers between devices, shards(): lax.all_gather(dpre_b, 'feat', axis=1, tiled=True)  83.7 us
    all_to_all x1, blocking collectives, shards(): lax.all_to_all(own_two[table], 'nodes', split_axis=0, concat_axis=0, tile...  57.9 us
    all_to_all x1, waiting for transfers between devices, shards(): lax.all_to_all(own_one[table], 'nodes', split_axis=0, concat_axis=0, tile...  50.7 us
    gather x2, local copies, waits for them, and re-layouts, gather_sources(): return flat[tile_src]  17.7 us
    ppermute x2, waiting for transfers between devices, shards(): lax.ppermute(logits, 'feat', [(dev, dev ^ hop) for dev in range(4)])  15.9 us
  transfers between devices with their start and end apart: 7, of which 6 were waited for; matrix products, arithmetic and copies ran while one was open for 0% of the time, Pallas kernels for 0%

profile of v1, /device:TPU:0, one launch (start us, length us, event | category | flops | bytes accessed | tf_op | source)
XLA Modules:
  0.0 623.2 jit_solution(9532484681822371420)
XLA Ops:
  7.2 0.0 copy-start
  7.2 0.7 compare_select_fusion.1
  7.9 0.1 copy.59
  8.0 0.1 reshape.111
  8.1 4.4 gather_fusion.1
  12.5 8.7 %all-to-all-start = ((bf16[32,2,128,256]{3,2,1,0:T(8,128)(2,1)}), bf16[32,2,128,256]{3,2,1,0:T(8,128)(2,1)}, u32[]{:S(2)}, u32[]{:S(2)}) async-start(bf16[32,2,128,256]{3,2,1,0:T(8,128)(2,1)} %bitcast.63), calls=%async_computation | async-start | bytes 8388608 | tf_op jit(solution)/shard_map/all_to_all | solution.py:29
  21.2 0.0 reduce-scatter.3.cloned.1.call-start
  21.2 0.0 copy-done.7
  21.3 0.1 copy.60
  21.3 0.1 reshape.119
  21.4 0.1 copy.56
  21.5 0.1 reshape.103
  21.7 0.0 copy-done.2
  21.7 1.2 gather_fusion
  22.9 0.1 reshape.102
  23.0 0.1 copy.57
  23.1 0.1 copy.58
  23.2 50.7 %all-to-all-done = bf16[32,2,128,256]{3,2,1,0:T(8,128)(2,1)} async-done(((bf16[32,2,128,256]{3,2,1,0:T(8,128)(2,1)}), bf16[32,2,128,256]{3,2,1,0:T(8,128)(2,1)}, u32[]{:S(2)}, u32[]{:S(2)}) %all-to-all-start) | async-done | bytes 4194336 | tf_op jit(solution)/shard_map/all_to_all | solution.py:29
  74.0 8.9 %gather_fusion.2 = bf16[128,128,256]{2,1,0:T(8,128)(2,1)} fusion(bf16[64,128,256]{2,1,0:T(8,128)(2,1)} %bitcast.4, s32[1024]{0:T(1024)S(1)} %pad_clamp_fusion), kind=kCustom, calls=%fused_computation.2 | custom fusion | bytes 16777728 | tf_op jit(solution)/shard_map/gather | solution.py:26
  82.9 6.5 %fusion = bf16[32,128,256]{2,1,0:T(8,128)(2,1)S(1)} fusion(bf16[32,128,256]{2,1,0:T(8,128)(2,1)S(1)} %bitcast.67, bf16[32,4,128,256]{3,2,1,0:T(8,128)(2,1)} %bitcast.65, bf16[32,4,128,128]{3,2,1,0:T(8,128)(2,1)} %param.13, bf16[32,4]{1,0:T(8,128)(2,1)S(1)} %copy.58), kind=kOutput, calls=%fused_computation.8 | convolution fusion | flops 1078984704 | bytes 16777472 | tf_op jit(solution)/shard_map/btij,btjf->bif/dot_general | solution.py:30
  89.3 1.3 copy-done.4
  90.7 8.1 %fusion.28 = f32[4096,1024]{1,0:T(8,128)} fusion(bf16[4096,256]{1,0:T(8,128)(2,1)S(1)} %bitcast.70, bf16[256,1024]{1,0:T(8,128)(2,1)S(1)} %copy-done), kind=kOutput, calls=%fused_computation.55 | convolution fusion | flops 2147483648 | bytes 19398656 | tf_op jit(solution)/shard_map/dot_general | solution.py:34
  98.7 0.0 reduce-scatter.3.cloned.1.call-update
  98.8 148.6 %reduce-scatter.3.cloned.1.call-done = f32[4096,256]{1,0:T(8,128)} async-done(((f32[4096,1024]{1,0:T(8,128)}), f32[4096,256]{1,0:T(8,128)}) %reduce-scatter.3.cloned.1.call-update) | async-done | bytes 4194320 | tf_op jit(solution)/shard_map/reduce_scatter | solution.py:35
  247.3 2.6 maximum_convert_fusion
  249.9 2.7 gather_fusion.3
  252.7 57.9 %all_to_all.15 = bf16[32,2,128,256]{3,2,1,0:T(8,128)(2,1)} all-to-all(bf16[32,2,128,256]{3,2,1,0:T(8,128)(2,1)} %bitcast.64), channel_id=1, replica_groups=mesh['nodes'=32,'feat'=4] {'nodes'}, dimensions={0} | all-to-all | bytes 8388608 | tf_op jit(solution)/shard_map/all_to_all | solution.py:39
  310.5 8.8 %gather_fusion.4 = bf16[128,128,256]{2,1,0:T(8,128)(2,1)} fusion(bf16[64,128,256]{2,1,0:T(8,128)(2,1)} %bitcast.61, s32[1024]{0:T(1024)S(1)} %pad_clamp_fusion), kind=kCustom, calls=%fused_computation.4 | custom fusion | bytes 16777728 | tf_op jit(solution)/shard_map/gather | solution.py:26
  319.3 6.5 %bitcast_add_fusion = f32[32,128,256]{2,1,0:T(8,128)S(1)} fusion(bf16[32,128,256]{2,1,0:T(8,128)(2,1)S(1)} %bitcast.59, bf16[32,4,128,256]{3,2,1,0:T(8,128)(2,1)} %bitcast.60, bf16[32,4,128,128]{3,2,1,0:T(8,128)(2,1)} %param.13, bf16[32,4]{1,0:T(8,128)(2,1)S(1)} %copy.58), kind=kOutput, calls=%fused_computation.6 | convolution fusion | flops 1077936128 | bytes 18874624 | tf_op jit(solution)/shard_map/btij,btjf->bif/dot_general | solution.py:41
  325.8 0.0 copy-start.5
  325.8 2.0 fusion.29
  327.8 0.3 collective-permute-start
  328.1 8.3 %collective-permute-done = f32[4096,16]{0,1:T(8,128)S(1)} collective-permute-done((f32[4096,16]{0,1:T(8,128)S(1)}, f32[4096,16]{0,1:T(8,128)S(1)}, u32[]{:S(2)}, u32[]{:S(2)}) %collective-permute-start) | collective-permute-done | bytes 262176 | tf_op jit(solution)/shard_map/ppermute | solution.py:54
  336.5 1.5 collective-permute-start.1
  338.0 0.1 copy.62
  338.1 0.1 eq.68
  338.2 7.6 %collective-permute-done.1 = f32[4096,16]{0,1:T(8,128)S(1)} collective-permute-done((f32[4096,16]{0,1:T(8,128)S(1)}, f32[4096,16]{0,1:T(8,128)S(1)}, u32[]{:S(2)}, u32[]{:S(2)}) %collective-permute-start.1) | collective-permute-done | bytes 262176 | tf_op jit(solution)/shard_map/ppermute | solution.py:54
  345.9 0.1 fusion.17
  345.9 0.1 convert_bitcast_fusion
  346.1 6.9 %fusion.1 = f32[32,4,128,16]{3,2,1,0:T(8,128)} fusion(bf16[32,4,128,128]{3,2,1,0:T(8,128)(2,1)} %param.13, bf16[32,4]{1,0:T(8,128)(2,1)S(1)} %copy.58, bf16[32,128,16,1]{1,0,2,3:T(8,128)(2,1)S(1)} %bitcast.72), kind=kOutput, calls=%fused_computation.10 | convolution fusion | flops 69206016 | bytes 5374208 | tf_op jit(solution)/shard_map/btij,bif->btjf/dot_general | solution.py:60
  353.0 8.7 %reshape.98 = f32[128,2048]{1,0:T(8,128)} reshape(f32[32,4,128,16]{3,2,1,0:T(8,128)} %fusion.1) | data formatting | bytes 2097152 | tf_op jit(solution)/shard_map/reshape | solution.py:66
  361.7 2.5 copy.65
  364.2 2.2 convolution_convert_fusion.1
  366.4 0.8 copy.67
  367.2 3.9 all-to-all-start.2
  371.1 0.3 all-gather.2.cloned.1.call-start
  371.4 0.1 copy.61
  371.5 0.1 eq.64
  371.6 8.5 %all-to-all-done.2 = bf16[32,2,128,16]{2,3,1,0:T(8,128)(2,1)S(1)} async-done(((bf16[32,2,128,16]{2,3,1,0:T(8,128)(2,1)}), bf16[32,2,128,16]{2,3,1,0:T(8,128)(2,1)S(1)}, u32[]{:S(2)}, u32[]{:S(2)}) %all-to-all-start.2) | async-done | bytes 262176 | tf_op jit(solution)/shard_map/all_to_all | solution.py:70
  380.0 1.7 copy.68
  381.8 4.7 reshape.99
  386.5 0.2 fusion.22
  386.6 2.0 reshape.100
  388.7 2.2 copy.69
  390.8 0.1 add_convert_fusion
  390.9 4.5 fusion.27
  395.4 0.0 all-gather.2.cloned.1.call-update
  395.5 0.0 reduce-scatter.5.cloned.1.call-start
  395.5 83.7 %all-gather.2.cloned.1.call-done = bf16[4096,1024]{1,0:T(8,128)(2,1)} async-done(((bf16[4096,256]{1,0:T(8,128)(2,1)}), bf16[4096,1024]{1,0:T(8,128)(2,1)}) %all-gather.2.cloned.1.call-update) | async-done | bytes 8388624 | tf_op jit(solution)/shard_map/all_gather | solution.py:94
  479.2 8.3 %convolution_convert_fusion = bf16[256,1024]{0,1:T(8,128)(2,1)} fusion(bf16[4096,256]{1,0:T(8,128)(2,1)} %bitcast.71, bf16[4096,1024]{1,0:T(8,128)(2,1)} %all-gather.2.cloned.1.call-done), kind=kOutput, calls=%fused_computation.19 | convolution fusion | flops 2147745792 | bytes 11010048 | tf_op jit(solution)/shard_map/dot_general | solution.py:92
  487.5 0.0 reduce-scatter.5.cloned.1.call-update
  487.5 0.4 fusion.30
  487.9 127.4 %all-reduce = (f32[256]{0:T(256)}, f32[256,16]{0,1:T(8,128)}) all-reduce(f32[256]{0:T(256)S(1)} %get-tuple-element.5, f32[256,16]{0,1:T(8,128)S(1)} %fusion.30), channel_id=1, replica_groups=mesh['nodes'=32,'feat'=4] {'nodes'}, use_global_device_ids=true, to_apply=%region_4.5 | all-reduce | flops 4352 | bytes 34816 | tf_op jit(solution)/shard_map/psum | solution.py:90
  615.3 1.3 convert_element_type.52
  (24 shorter events, 0.1 us)
Async XLA Ops:
  7.2 83.5 %copy-start = (bf16[256,1024]{1,0:T(8,128)(2,1)S(1)}, bf16[256,1024]{1,0:T(8,128)(2,1)}, u32[]{:S(2)}) copy-start(bf16[256,1024]{1,0:T(8,128)(2,1)} %param.15) | copy-start | bytes 1572868
  12.5 8.7 %copy-start.7 = (s32[32,4]{0,1:T(4,128)S(1)}, s32[32,4]{0,1:T(4,128)}, u32[]{:S(2)}) copy-start(s32[32,4]{0,1:T(4,128)} %param.12) | copy-start | bytes 1540
  12.5 9.2 %copy-start.2 = (s32[1,32]{1,0:T(1,128)S(1)}, s32[1,32]{1,0:T(1,128)}, u32[]{:S(2)}) copy-start(s32[1,32]{1,0:T(1,128)} %param.10) | copy-start | bytes 388
  12.5 61.5 %all-to-all-start = ((bf16[32,2,128,256]{3,2,1,0:T(8,128)(2,1)}), bf16[32,2,128,256]{3,2,1,0:T(8,128)(2,1)}, u32[]{:S(2)}, u32[]{:S(2)}) async-start(bf16[32,2,128,256]{3,2,1,0:T(8,128)(2,1)} %bitcast.63), calls=%async_computation | async-start | bytes 8388608 | tf_op jit(solution)/shard_map/all_to_all | solution.py:29
  21.2 226.1 %reduce-scatter.3.cloned.1.call-start = ((), (), s32[]{:S(2)}) async-start(), calls=%async_computation.5 | async-start | bytes 20971520 | tf_op jit(solution)/shard_map/reduce_scatter | solution.py:35
  74.0 8.9 %copy-start.3 = (bf16[4096,256]{1,0:T(8,128)(2,1)S(1)}, bf16[4096,256]{1,0:T(8,128)(2,1)}, u32[]{:S(2)}) copy-start(bf16[4096,256]{1,0:T(8,128)(2,1)} %param.9) | copy-start | bytes 6291460
  89.3 1.3 copy-start.4
  98.7 148.6 %copy-start.9 = (f32[256]{0:T(256)S(1)}, f32[256]{0:T(256)}, u32[]{:S(2)}) copy-start(f32[256]{0:T(256)} %param.16) | copy-start | bytes 3076
  319.3 6.5 %copy-start.6 = (bf16[256,16]{0,1:T(8,128)(2,1)S(1)}, bf16[256,16]{0,1:T(8,128)(2,1)}, u32[]{:S(2)}) copy-start(bf16[256,16]{0,1:T(8,128)(2,1)} %param.17) | copy-start | bytes 24580
  325.8 20.1 %copy-start.5 = (s32[4096]{0:T(1024)S(1)}, s32[4096]{0:T(1024)}, u32[]{:S(2)}) copy-start(s32[4096]{0:T(1024)} %param.14) | copy-start | bytes 49156
  327.8 8.6 %collective-permute-start = (f32[4096,16]{0,1:T(8,128)S(1)}, f32[4096,16]{0,1:T(8,128)S(1)}, u32[]{:S(2)}, u32[]{:S(2)}) collective-permute-start(f32[4096,16]{0,1:T(8,128)S(1)} %fusion.29), channel_id=1, source_target_pairs={{0,1},{1,0},{2,3},{3,2},{4,5},{5,4},{6,7},{7,6},{8,9},{9,8},{10,11... | collective-permute-start | bytes 786440 | tf_op jit(solution)/shard_map/ppermute | solution.py:54
  336.5 9.4 %collective-permute-start.1 = (f32[4096,16]{0,1:T(8,128)S(1)}, f32[4096,16]{0,1:T(8,128)S(1)}, u32[]{:S(2)}, u32[]{:S(2)}) collective-permute-start(f32[4096,16]{0,1:T(8,128)S(1)} %add.72), channel_id=1, source_target_pairs={{0,2},{1,3},{2,0},{3,1},{4,6},{5,7},{6,4},{7,5},{8,10},{9,11},{10,... | collective-permute-start | bytes 786440 | tf_op jit(solution)/shard_map/ppermute | solution.py:54
  361.7 9.7 %copy-start.8 = (s32[1,32,2]{1,2,0:T(2,128)S(1)}, s32[1,32,2]{1,2,0:T(2,128)}, u32[]{:S(2)}) copy-start(s32[1,32,2]{1,2,0:T(2,128)} %param.11) | copy-start | bytes 772
  367.2 12.8 %all-to-all-start.2 = ((bf16[32,2,128,16]{2,3,1,0:T(8,128)(2,1)}), bf16[32,2,128,16]{2,3,1,0:T(8,128)(2,1)S(1)}, u32[]{:S(2)}, u32[]{:S(2)}) async-start(bf16[32,2,128,16]{2,3,1,0:T(8,128)(2,1)} %copy.67), calls=%async_computation.3 | async-start | bytes 524288 | tf_op jit(solution)/shard_map/all_to_all | solution.py:70
  371.1 108.1 %all-gather.2.cloned.1.call-start = ((), (), s32[]{:S(2)}) async-start(), calls=%async_computation.6 | async-start | bytes 10485760 | tf_op jit(solution)/shard_map/all_gather | solution.py:94
  395.5 219.8 %reduce-scatter.5.cloned.1.call-start = ((), (), s32[]{:S(2)}) async-start(), calls=%async_computation.7 | async-start | bytes 540672 | tf_op jit(solution)/shard_map/reduce_scatter | solution.py:98
  479.2 137.4 %copy-start.1 = (bf16[256,1024]{1,0:T(8,128)(2,1)S(1)}, bf16[256,1024]{1,0:T(8,128)(2,1)}, u32[]{:S(2)}) copy-start(bf16[256,1024]{1,0:T(8,128)(2,1)} %param.15) | copy-start | bytes 1572868
Sparse Core Ops, SparseCore 0:
  98.9 148.3 reduce-scatter.2
  395.6 83.5 all-gather.1
  487.6 77.6 reduce-scatter.4
